TPU v7x, 32 devices: a whole 2x2x4 slice. The times are simulated.
32 devices in a mesh: dp: 4 (over z), row: 2 (over x), col: 4 (over y, core).
Axes of the slice: x: 2, y: 2, z: 4, core: 2. Of those that a mesh axis runs over, the one named last changes fastest.
Arguments:
- inputs: bfloat16 [16384, 768], P(('dp', 'row', 'col')), may hold values from -6 to 6
- pre_attn_gain: bfloat16 [768], replicated, may hold values from 0.25 to 1.75
- pre_attn_shift: bfloat16 [768], replicated, may hold values from -1.75 to 1.75
- qkv_weight: bfloat16 [768, 3, 768], P('row', None, 'col'), may hold values from -0.3125 to 0.3125
- qv_bias: bfloat16 [2, 768], P(None, 'col'), may hold values from -3 to 3
- out_weight: bfloat16 [768, 768], P('col', 'row'), may hold values from -1.75 to 1.75
- out_bias: bfloat16 [768], replicated, may hold values from -1.75 to 1.75
- pre_mlp_gain: bfloat16 [768], replicated, may hold values from 0.25 to 1.75
- pre_mlp_shift: bfloat16 [768], replicated, may hold values from -1.75 to 1.75
- fc_weight: bfloat16 [768, 3072], P('row', 'col'), may hold values from -0.21875 to 0.21875
- fc_bias: bfloat16 [3072], P('col'), may hold values from -3 to 3
- proj_weight: bfloat16 [3072, 768], P('col', 'row'), may hold values from -0.109375 to 0.109375
- proj_bias: bfloat16 [768], replicated, may hold values from -1.75 to 1.75
- cotangent: bfloat16 [16384, 768], P(('dp', 'row', 'col')), may hold values from -6 to 6
Outputs:
- block_out: bfloat16 [16384, 768], P(('dp', 'row', 'col'))
- input_grad: bfloat16 [16384, 768], P(('dp', 'row', 'col'))
- grad_pre_attn_gain: float32 [768], replicated
- grad_pre_attn_shift: float32 [768], replicated
- grad_qkv_weight: float32 [768, 3, 768], P('row', None, 'col')
- grad_qv_bias: float32 [2, 768], P(None, 'col')
- grad_out_weight: float32 [768, 768], P('col', 'row')
- grad_out_bias: float32 [768], replicated
- grad_pre_mlp_gain: float32 [768], replicated
- grad_pre_mlp_shift: float32 [768], replicated
- grad_fc_weight: float32 [768, 3072], P('row', 'col')
- grad_fc_bias: float32 [3072], P('col')
- grad_proj_weight: float32 [3072, 768], P('col', 'row')
- grad_proj_bias: float32 [768], replicated
All inputs are finite; a program needn't handle non-finite values.
Results may differ from a plain program's by a relative error of at most 0.013.
The roundings to bfloat16 on the way count: a program that leaves them out, or rounds other values in their place, can miss the bound.
Values may be sent and summed in bfloat16 or wider, within the bound.
No kernel may reach another device: no remote copies, remote signals or barrier semaphores. Data moves between devices by JAX's collectives and lax.ppermute only.
A program may use at most 128 MiB of HBM per device.

v0:
```python
import jax
import jax.numpy as jnp
from jax import lax
from jax.sharding import PartitionSpec as P

HEAD_DIM = 64
SEQ_LEN = 2048


eps = 1e-05
masked_score = -1e30


def layer_norm(rows, gain, shift):
    average = jnp.mean(rows, axis=-1, keepdims=True)
    centred = rows - average
    variance = jnp.mean(centred * centred, axis=-1, keepdims=True)
    return centred * lax.rsqrt(variance + eps) * gain + shift


def gelu_tanh(values):
    return jax.nn.gelu(values, approximate=True)


def masked_scores(query_block, keys_seq, first_row, score_scale):
    scores = (
        jnp.einsum("qhd,khd->hqk", query_block, keys_seq, preferred_element_type=jnp.float32)
        * score_scale
    )
    query_pos = first_row + jnp.arange(query_block.shape[0], dtype=jnp.int32)
    key_pos = jnp.arange(keys_seq.shape[0], dtype=jnp.int32)
    allowed = key_pos[None, :] <= query_pos[:, None]
    return jnp.where(allowed[None], scores, masked_score)


def attend_forward(queries, keys_all, values_all, block_rows, score_scale):
    seq_count, seq_len, heads_here, head_dim = queries.shape
    blocks = seq_len // block_rows

    def attend_one_block(block_index):
        seq_index = block_index // blocks
        first_row = block_index % blocks * block_rows
        query_block = lax.dynamic_slice(
            queries, (seq_index, first_row, 0, 0), (1, block_rows, heads_here, head_dim)
        )[0]
        keys_seq = lax.dynamic_index_in_dim(keys_all, seq_index, 0, keepdims=False)
        values_seq = lax.dynamic_index_in_dim(values_all, seq_index, 0, keepdims=False)
        scores = masked_scores(query_block, keys_seq, first_row, score_scale)
        row_max = jnp.max(scores, axis=-1, keepdims=True)
        shifted = jnp.exp(scores - row_max)
        row_total = jnp.sum(shifted, axis=-1, keepdims=True)
        attn_probs = (shifted / row_total).astype(jnp.bfloat16)
        context = jnp.einsum(
            "hqk,khd->qhd", attn_probs, values_seq, preferred_element_type=jnp.float32
        )
        log_total = (row_max + jnp.log(row_total))[..., 0]
        return (context.astype(jnp.bfloat16), log_total)

    return lax.map(attend_one_block, jnp.arange(seq_count * blocks, dtype=jnp.int32))


def attend_backward(
    queries, keys_all, values_all, context_grad, log_totals, block_rows, score_scale
):
    seq_count, seq_len, heads_here, head_dim = queries.shape
    blocks = seq_len // block_rows
    lse_seq = log_totals.reshape(seq_count, blocks, heads_here, block_rows)

    def one_sequence(seq_index):
        keys_seq = lax.dynamic_index_in_dim(keys_all, seq_index, 0, keepdims=False)
        values_seq = lax.dynamic_index_in_dim(values_all, seq_index, 0, keepdims=False)

        def one_one_block(running, block_index):
            key_grad, value_grad = running
            first_row = block_index * block_rows
            block_shape = (1, block_rows, heads_here, head_dim)
            query_block = lax.dynamic_slice(queries, (seq_index, first_row, 0, 0), block_shape)[0]
            out_block = lax.dynamic_slice(context_grad, (seq_index, first_row, 0, 0), block_shape)[
                0
            ]
            block_lse = lax.dynamic_slice(
                lse_seq, (seq_index, block_index, 0, 0), (1, 1, heads_here, block_rows)
            )[0, 0]
            scores = masked_scores(query_block, keys_seq, first_row, score_scale)
            probs_exact = jnp.exp(scores - block_lse[..., None])
            value_grad = value_grad + jnp.einsum(
                "hqk,qhd->khd",
                probs_exact.astype(jnp.bfloat16),
                out_block,
                preferred_element_type=jnp.float32,
            )
            prob_grad = jnp.einsum(
                "qhd,khd->hqk", out_block, values_seq, preferred_element_type=jnp.float32
            )
            inner_sum = jnp.sum(probs_exact * prob_grad, axis=-1, keepdims=True)
            score_grad = (probs_exact * (prob_grad - inner_sum)).astype(jnp.bfloat16)
            query_grad = (
                jnp.einsum("hqk,khd->qhd", score_grad, keys_seq, preferred_element_type=jnp.float32)
                * score_scale
            )
            key_grad = (
                key_grad
                + jnp.einsum(
                    "hqk,qhd->khd", score_grad, query_block, preferred_element_type=jnp.float32
                )
                * score_scale
            )
            return ((key_grad, value_grad), query_grad)

        empty_grad = jnp.zeros((seq_len, heads_here, head_dim), jnp.float32)
        (key_grad, value_grad), query_grads = lax.scan(
            one_one_block, (empty_grad, empty_grad), jnp.arange(blocks, dtype=jnp.int32)
        )
        return (query_grads.reshape(seq_len, heads_here, head_dim), key_grad, value_grad)

    return lax.map(one_sequence, jnp.arange(seq_count, dtype=jnp.int32))


def body(
    inputs,
    pre_attn_gain,
    pre_attn_shift,
    qkv_weight,
    qv_bias,
    out_weight,
    out_bias,
    pre_mlp_gain,
    pre_mlp_shift,
    fc_weight,
    fc_bias,
    proj_weight,
    proj_bias,
    cotangent,
):
    tok_rows, model_width = inputs.shape
    col_count = lax.axis_size("col")
    row_count = lax.axis_size("row")
    col_index = lax.axis_index("col")
    group_rows = tok_rows * col_count
    head_cols = qkv_weight.shape[2]
    hidden_cols = fc_weight.shape[1]
    hidden_all = hidden_cols * col_count
    heads_here = head_cols // HEAD_DIM
    seq_count = group_rows // SEQ_LEN
    block_rows = min(512, SEQ_LEN)
    score_scale = HEAD_DIM ** (-0.5)
    split_shape = (seq_count, SEQ_LEN, heads_here, HEAD_DIM)
    gain_one = pre_attn_gain.astype(jnp.float32)
    shift_one = pre_attn_shift.astype(jnp.float32)
    gain_two = pre_mlp_gain.astype(jnp.float32)
    shift_two = pre_mlp_shift.astype(jnp.float32)
    qkv_full, out_full = (
        lax.all_gather(qkv_weight, "row", axis=0, tiled=True),
        lax.all_gather(out_weight, "row", axis=1, tiled=True),
    )
    fc_grid, proj_grid, fc_bias_grid = (
        lax.all_gather(fc_weight[None], ("row", "col"), axis=0, tiled=True),
        lax.all_gather(proj_weight[None], ("row", "col"), axis=0, tiled=True),
        lax.all_gather(fc_bias[None], ("row", "col"), axis=0, tiled=True),
    )
    stream = inputs.astype(jnp.float32)
    normed_one = layer_norm(stream, gain_one, shift_one).astype(jnp.bfloat16)
    normed_all = lax.all_gather(normed_one, "col", axis=0, tiled=True)
    qkv_raw = jnp.einsum("td,dje->tje", normed_all, qkv_full, preferred_element_type=jnp.float32)
    bias_wide = qv_bias.astype(jnp.float32)
    bias_rows = jnp.stack([bias_wide[0], jnp.zeros_like(bias_wide[0]), bias_wide[1]])
    qkv_low = (qkv_raw + bias_rows).astype(jnp.bfloat16)
    queries = qkv_low[:, 0].reshape(split_shape)
    keys_all = qkv_low[:, 1].reshape(split_shape)
    values_all = qkv_low[:, 2].reshape(split_shape)
    contexts, log_totals = attend_forward(queries, keys_all, values_all, block_rows, score_scale)
    context = contexts.reshape(group_rows, head_cols)
    attn_sum = lax.psum_scatter(
        jnp.dot(context, out_full, preferred_element_type=jnp.float32),
        "col",
        scatter_dimension=0,
        tiled=True,
    )
    mid_stream = stream + attn_sum + out_bias.astype(jnp.float32)
    normed_two = layer_norm(mid_stream, gain_two, shift_two).astype(jnp.bfloat16)
    fc_blocks = fc_grid.reshape(row_count, col_count, fc_weight.shape[0], hidden_cols)
    proj_blocks = proj_grid.reshape(row_count, col_count, hidden_cols, proj_weight.shape[1])
    fc_bias_all = (
        fc_bias_grid.reshape(row_count, col_count, hidden_cols)[0]
        .reshape(hidden_all)
        .astype(jnp.float32)
    )
    normed_split = normed_two.reshape(tok_rows, row_count, -1)
    pre_act = (
        jnp.einsum(
            "trd,rcdf->tcf", normed_split, fc_blocks, preferred_element_type=jnp.float32
        ).reshape(tok_rows, hidden_all)
        + fc_bias_all
    )
    hidden_low = gelu_tanh(pre_act).astype(jnp.bfloat16)
    hidden_split = hidden_low.reshape(tok_rows, col_count, hidden_cols)
    mlp_out = jnp.einsum(
        "tcf,rcfd->trd", hidden_split, proj_blocks, preferred_element_type=jnp.float32
    ).reshape(tok_rows, model_width)
    block_out = (mid_stream + mlp_out + proj_bias.astype(jnp.float32)).astype(jnp.bfloat16)
    out_grad = cotangent.astype(jnp.float32)
    proj_bias_grad = jnp.sum(out_grad, axis=0)
    gelu_pull = jax.vjp(gelu_tanh, pre_act)[1]
    cot_split = cotangent.reshape(tok_rows, row_count, -1)
    hidden_grad = jnp.einsum(
        "trd,rcfd->tcf", cot_split, proj_blocks, preferred_element_type=jnp.float32
    ).reshape(tok_rows, hidden_all)
    proj_grid_grad = jnp.einsum(
        "tcf,trd->rcfd", hidden_split, cot_split, preferred_element_type=jnp.float32
    )
    pre_grad = gelu_pull(hidden_grad)[0].astype(jnp.bfloat16)
    fc_bias_grad = jnp.sum(pre_grad, axis=0, dtype=jnp.float32)
    pre_split = pre_grad.reshape(tok_rows, col_count, hidden_cols)
    fc_grid_grad = jnp.einsum(
        "trd,tcf->rcdf", normed_split, pre_split, preferred_element_type=jnp.float32
    )
    normed_two_grad = jnp.einsum(
        "tcf,rcdf->trd", pre_split, fc_blocks, preferred_element_type=jnp.float32
    ).reshape(tok_rows, model_width)
    fc_part, proj_part = (
        lax.psum_scatter(
            fc_grid_grad.reshape(row_count * col_count, -1, hidden_cols),
            ("row", "col"),
            scatter_dimension=0,
            tiled=True,
        ),
        lax.psum_scatter(
            proj_grid_grad.reshape(row_count * col_count, hidden_cols, -1),
            ("row", "col"),
            scatter_dimension=0,
            tiled=True,
        ),
    )
    fc_block_grad = fc_part[0]
    proj_block_grad = proj_part[0]
    norm_two_pull = jax.vjp(layer_norm, mid_stream, gain_two, shift_two)[1]
    stream_two, gain_two_grad, shift_two_grad = norm_two_pull(normed_two_grad)
    mid_grad = out_grad + stream_two
    mid_low = mid_grad.astype(jnp.bfloat16)
    out_bias_grad = jnp.sum(mid_low, axis=0, dtype=jnp.float32)
    mid_all = lax.all_gather(mid_low, "col", axis=0, tiled=True)
    context_grad = jnp.einsum(
        "td,ed->te", mid_all, out_full, preferred_element_type=jnp.float32
    ).astype(jnp.bfloat16)
    out_full_grad = jnp.einsum("te,td->ed", context, mid_all, preferred_element_type=jnp.float32)
    query_grads, key_grads, value_grads = attend_backward(
        queries,
        keys_all,
        values_all,
        context_grad.reshape(split_shape),
        log_totals,
        block_rows,
        score_scale,
    )
    qkv_grad = jnp.stack(
        [
            query_grads.reshape(group_rows, head_cols),
            key_grads.reshape(group_rows, head_cols),
            value_grads.reshape(group_rows, head_cols),
        ],
        axis=1,
    ).astype(jnp.bfloat16)
    bias_block = jnp.sum(qkv_grad[:, 0::2], axis=0, dtype=jnp.float32)
    qv_grad_wide = lax.dynamic_update_slice_in_dim(
        jnp.zeros((2, model_width), jnp.float32), bias_block, col_index * head_cols, 1
    )
    qkv_full_grad = jnp.einsum(
        "td,tje->dje", normed_all, qkv_grad, preferred_element_type=jnp.float32
    )
    normed_one_grad = lax.psum_scatter(
        jnp.einsum("tje,dje->td", qkv_grad, qkv_full, preferred_element_type=jnp.float32),
        "col",
        scatter_dimension=0,
        tiled=True,
    )
    norm_one_pull = jax.vjp(layer_norm, stream, gain_one, shift_one)[1]
    stream_one, gain_one_grad, shift_one_grad = norm_one_pull(normed_one_grad)
    input_grad = (mid_grad + stream_one).astype(jnp.bfloat16)
    qkv_block_grad, out_block_grad = (
        lax.psum_scatter(qkv_full_grad, "row", scatter_dimension=0, tiled=True),
        lax.psum_scatter(out_full_grad, "row", scatter_dimension=1, tiled=True),
    )
    qkv_sum, out_sum, fc_sum, proj_sum = lax.psum(
        (qkv_block_grad, out_block_grad, fc_block_grad, proj_block_grad), "dp"
    )
    vector_grads = jnp.stack(
        [
            gain_one_grad,
            shift_one_grad,
            out_bias_grad,
            gain_two_grad,
            shift_two_grad,
            proj_bias_grad,
        ]
    )
    vector_sum, qv_sum, fc_bias_sum = lax.psum(
        (vector_grads, qv_grad_wide, fc_bias_grad), ("dp", "row", "col")
    )
    qv_own = lax.dynamic_slice_in_dim(qv_sum, col_index * head_cols, head_cols, 1)
    fc_bias_own = lax.dynamic_slice_in_dim(fc_bias_sum, col_index * hidden_cols, hidden_cols, 0)
    return (
        block_out,
        input_grad,
        vector_sum[0],
        vector_sum[1],
        qkv_sum,
        qv_own,
        out_sum,
        vector_sum[2],
        vector_sum[3],
        vector_sum[4],
        fc_sum,
        fc_bias_own,
        proj_sum,
        vector_sum[5],
    )


def solution(mesh):
    placed = (
        P(("dp", "row", "col"), None),
        P(),
        P(),
        P("row", None, "col"),
        P(None, "col"),
        P("col", "row"),
        P(),
        P(),
        P(),
        P("row", "col"),
        P("col"),
        P("col", "row"),
        P(),
        P(("dp", "row", "col"), None),
    )
    return jax.shard_map(
        body,
        mesh=mesh,
        in_specs=placed,
        out_specs=(
            P(("dp", "row", "col"), None),
            P(("dp", "row", "col"), None),
            P(),
            P(),
            P("row", None, "col"),
            P(None, "col"),
            P("col", "row"),
            P(),
            P(),
            P(),
            P("row", "col"),
            P("col"),
            P("col", "row"),
            P(),
        ),
        check_vma=False,
    )
```

profile of v0, /device:TPU:0, one launch (start us, length us, event | category | flops | bytes accessed | tf_op | source)
XLA Modules:
  0.0 853.6 jit_solution(10407130782466169802)
XLA Ops:
  15.4 7.5 all_gather.23
  22.8 12.0 %all_gather.22 = bf16[768,3,192]{0,2,1:T(8,128)(2,1)S(1)} all-gather(bf16[384,3,192]{0,2,1:T(8,128)(2,1)S(1)} %copy-done.31), channel_id=1, replica_groups=mesh['dp'=4,'row'=2,'col'=4] {'row'}, dimensions={0}, use_global_device_ids=true | all-gather | bytes 1327104 | tf_op jit(solution)/shard_map/all_gather | solution.py:153
  35.0 10.9 %all-gather.9.cloned.1.call-done = bf16[2048,768]{1,0:T(8,128)(2,1)} async-done(((bf16[512,768]{1,0:T(8,128)(2,1)}), bf16[2048,768]{1,0:T(8,128)(2,1)}) %all-gather.9.cloned.1.call-update) | async-done | bytes 3145744 | tf_op jit(solution)/shard_map/all_gather | solution.py:163
  50.4 93.9 %while.41 = (s32[]{:T(128)}, bf16[4,512,3,64]{1,3,2,0:T(8,128)(2,1)}, f32[4,3,512]{2,1,0:T(4,128)S(1)}, s32[4]{0:T(128)S(1)}, bf16[1,2048,3,64]{1,3,2,0:T(8,128)...) while((s32[]{:T(128)}, ...), condition=%wide.region_5.6_spmd, body=%wide.region_2.5_spmd.sunk | while | flops 844200960 | bytes 43968828 | solution.py:59
  59.7 6.8 fusion.140
  66.4 7.8 fusion.141
  83.6 6.8 fusion.140
  90.4 7.3 fusion.141
  106.9 6.8 fusion.140
  113.7 7.3 fusion.141
  130.3 6.8 fusion.140
  137.0 7.3 fusion.141
  151.1 9.1 %all-gather.3 = bf16[8,1,768]{2,1,0:T(2,128)(2,1)S(1)} all-gather(bf16[1,1,768]{2,1,0:T(2,128)(2,1)S(1)} %reshape.265), channel_id=3, replica_groups=mesh['dp'=4,'row'=2,'col'=4] {'row','col'}, dimensions={0}, use_global_device_ids=true | all-gather | bytes 13824 | tf_op jit(solution)/shard_map/all_gather | solution.py:159
  165.6 6.7 copy.56
  172.3 36.3 %reduce-scatter.7.cloned.1.call-done = f32[512,768]{1,0:T(8,128)} async-done(((f32[2048,768]{1,0:T(8,128)}), f32[512,768]{1,0:T(8,128)}) %reduce-scatter.7.cloned.1.call-update) | async-done | bytes 1572880 | tf_op jit(solution)/shard_map/reduce_scatter | solution.py:173
  212.8 6.2 multiply_convert_fusion.1
  219.0 30.4 %all-gather.15.cloned.1.call-done = bf16[6144,384]{1,0:T(8,128)(2,1)} async-done(((bf16[768,384]{1,0:T(8,128)(2,1)}), bf16[6144,384]{1,0:T(8,128)(2,1)}) %all-gather.15.cloned.1.call-update) | async-done | bytes 4718608 | tf_op jit(solution)/shard_map/all_gather | solution.py:158
  249.4 9.7 %convert_reduce_fusion = (f32[3072]{0:T(1024)}, bf16[512,3072]{1,0:T(8,128)(2,1)S(1)}) fusion(f32[3072]{0:T(1024)S(1)} %bitcast.274, f32[512,3072,1]{1,0,2:T(8,128)} %get-tuple-element.320, bf16[3072,384,2]{1,0,2:T(8,128)(2,1)} %bitcast.248, bf16[64,2,8,384]{3,2,1,0:T(8,128)(2,1)S(1)} %bitcast.258), kind=kOutput, calls=%fused_computation.68 | convolution fusion | flops 2452091904 | bytes 14966784 | tf_op jit(solution)/shard_map/trd,rcfd->tcf/dot_general | solution.py:205
  259.1 7.0 fusion.74
  269.9 28.6 %all-gather.11.cloned.1.call-done = bf16[2048,768]{1,0:T(8,128)(2,1)} async-done(((bf16[512,768]{1,0:T(8,128)(2,1)}), bf16[2048,768]{1,0:T(8,128)(2,1)}) %all-gather.11.cloned.1.call-update) | async-done | bytes 3145744 | tf_op jit(solution)/shard_map/all_gather | solution.py:241
  305.1 138.4 %while.42 = (s32[]{:T(128)}, f32[2048,3,64]{0,2,1:T(8,128)}, f32[2048,3,64]{0,2,1:T(8,128)}, bf16[4,512,3,64]{1,3,2,0:T(8,128)(2,1)}, s32[4]{0:T(128)S(1)}, /*in...) while((s32[]{:T(128)}, f32[2048,3,64]{0,2,1:T(8,128)}, ...), condition=%wide.region_13.14_spmd.clone, body=%wide.region_11.13_spmd.clone.sunk | while | flops 2063563776 | bytes 156680720 | solution.py:111
  452.0 6.8 reshape.247
  458.9 8.2 convolution_bitcast_fusion.2
  467.1 9.7 %copy.66 = f32[2,4,384,768]{3,2,1,0:T(8,128)} copy(f32[2,4,384,768]{2,3,0,1:T(8,128)} %convolution_bitcast_fusion.2) | data formatting | bytes 18874368 | tf_op jit(solution)/shard_map/trd,tcf->rcdf/transpose | solution.py:214
  476.9 7.1 reshape.244
  501.1 59.7 %reduce-scatter.15.cloned.1.call-done = f32[1,384,768]{2,1,0:T(8,128)} async-done(((f32[8,384,768]{2,1,0:T(8,128)}), f32[1,384,768]{2,1,0:T(8,128)}) %reduce-scatter.15.cloned.1.call-update) | async-done | bytes 1179664 | tf_op jit(solution)/shard_map/reduce_scatter | solution.py:221
  560.8 80.4 %reduce-scatter.17.cloned.1.call-done = f32[1,768,384]{2,1,0:T(8,128)} async-done(((f32[8,768,384]{2,1,0:T(8,128)}), f32[1,768,384]{2,1,0:T(8,128)}) %reduce-scatter.17.cloned.1.call-update) | async-done | bytes 1179664 | tf_op jit(solution)/shard_map/reduce_scatter | solution.py:227
  641.3 6.8 copy.58
  648.2 8.4 fusion.76
  657.1 45.1 %reduce-scatter.9.cloned.1.call-done = f32[512,768]{1,0:T(8,128)} async-done(((f32[2048,768]{1,0:T(8,128)}), f32[512,768]{1,0:T(8,128)}) %reduce-scatter.9.cloned.1.call-update) | async-done | bytes 1572880 | tf_op jit(solution)/shard_map/reduce_scatter | solution.py:270
  706.7 43.7 %all-reduce = (f32[6,768]{1,0:T(8,128)S(1)}, f32[2,768]{1,0:T(2,128)S(1)}, f32[3072]{0:T(1024)S(1)}) all-reduce(f32[6,768]{1,0:T(8,128)S(1)} %stack.24, f32[2,768]{1,0:T(2,128)S(1)} %dynamic_update_slice.29, f32[3072]{0:T(1024)S(1)} %copy-done.44), channel_id=1, replica_groups=mesh['dp'=4,'row'=2,'col'=4] {'dp','row','col'}, use_global_device_ids=true, to_apply=%region_23.24 | all-reduce | flops 9216 | bytes 73728 | tf_op jit(solution)/shard_map/psum | solution.py:296
  752.4 88.2 %all-reduce.4.cloned.1.call-done = (f32[384,3,192]{0,2,1:T(8,128)}, f32[192,384]{1,0:T(8,128)}, f32[384,768]{1,0:T(8,128)}, f32[768,384]{1,0:T(8,128)}) async-done(((f32[384,3,192]{0,2,1:T(8,128)}, f32[192,384]{1,0:T(8,128)}, f32[384,768]{1,0:T(8,128)}, f32[768,384]{1,0:T(8,128)}), (f32[384,3,192]{0,2,1:T(8,128)}, f32[192,384]{1,0:T(8,128)}, f32[384,768]{1,0:T(8,128)}, ...) | async-done | bytes 3538960 | tf_op jit(solution)/shard_map/psum | solution.py:283
  (313 shorter events, 233.8 us)
Async XLA Ops:
  7.2 8.1 copy-start.47
  7.2 8.2 copy-start.32
  7.2 15.6 %copy-start.31 = (bf16[384,3,192]{0,2,1:T(8,128)(2,1)S(1)}, bf16[384,3,192]{0,2,1:T(8,128)(2,1)}, u32[]{:S(2)}) copy-start(bf16[384,3,192]{0,2,1:T(8,128)(2,1)} %param.21) | copy-start | bytes 1327108
  7.2 38.7 %all-gather.9.cloned.1.call-start = ((), (), s32[]{:S(2)}) async-start(), calls=%async_computation.6 | async-start | bytes 3932160 | tf_op jit(solution)/shard_map/all_gather | solution.py:163
  14.5 145.7 %all-gather.13.cloned.1.call-start = ((), (), s32[]{:S(2)}) async-start(), calls=%async_computation.14 | async-start | bytes 5308416 | tf_op jit(solution)/shard_map/all_gather | solution.py:157
  15.3 193.3 %reduce-scatter.7.cloned.1.call-start = ((), (), s32[]{:S(2)}) async-start(), calls=%async_computation.7 | async-start | bytes 7864320 | tf_op jit(solution)/shard_map/reduce_scatter | solution.py:173
  34.9 15.0 %copy-start.28 = (bf16[768,3,192]{0,2,1:T(8,128)(2,1)}, bf16[768,3,192]{0,2,1:T(8,128)(2,1)S(1)}, u32[]{:S(2)}) copy-start(bf16[768,3,192]{0,2,1:T(8,128)(2,1)S(1)} %all_gather.22) | copy-start | bytes 2654212
  150.3 99.1 %all-gather.15.cloned.1.call-start = ((), (), s32[]{:S(2)}) async-start(), calls=%async_computation.15 | async-start | bytes 5308416 | tf_op jit(solution)/shard_map/all_gather | solution.py:158
  150.9 147.6 %all-gather.11.cloned.1.call-start = ((), (), s32[]{:S(2)}) async-start(), calls=%async_computation.8 | async-start | bytes 3932160 | tf_op jit(solution)/shard_map/all_gather | solution.py:241
  165.6 43.0 %copy-start.7 = (bf16[512,768]{1,0:T(8,128)(2,1)S(1)}, bf16[512,768]{1,0:T(8,128)(2,1)}, u32[]{:S(2)}) copy-start(bf16[512,768]{1,0:T(8,128)(2,1)} %param.18) | copy-start | bytes 2359300
  212.8 36.6 %copy-start.20 = (bf16[512,768]{1,0:T(8,128)(2,1)S(1)}, bf16[512,768]{1,0:T(8,128)(2,1)}, u32[]{:S(2)}) copy-start(bf16[512,768]{1,0:T(8,128)(2,1)} %param.31) | copy-start | bytes 2359300
  249.4 9.7 %copy-start.10 = (f32[512,768]{1,0:T(8,128)S(1)}, f32[512,768]{1,0:T(8,128)}, u32[]{:S(2)}) copy-start(f32[512,768]{1,0:T(8,128)} %copy-done.9) | copy-start | bytes 4718596
  269.8 231.2 %reduce-scatter.13.cloned.1.call-start = ((), (), s32[]{:S(2)}) async-start(), calls=%async_computation.11 | async-start | bytes 884736 | tf_op jit(solution)/shard_map/reduce_scatter | solution.py:281
  302.0 199.1 %reduce-scatter.11.cloned.1.call-start = ((), (), s32[]{:S(2)}) async-start(), calls=%async_computation.10 | async-start | bytes 2654208 | tf_op jit(solution)/shard_map/reduce_scatter | solution.py:280
  305.3 7.1 copy-start.2
  305.3 7.1 copy-start.5
  305.4 7.1 copy-start.24
  338.3 7.1 copy-start.2
  452.0 108.8 %reduce-scatter.15.cloned.1.call-start = ((), (), s32[]{:S(2)}) async-start(), calls=%async_computation.12 | async-start | bytes 10616832 | tf_op jit(solution)/shard_map/reduce_scatter | solution.py:221
  476.8 164.4 %reduce-scatter.17.cloned.1.call-start = ((), (), s32[]{:S(2)}) async-start(), calls=%async_computation.13 | async-start | bytes 10616832 | tf_op jit(solution)/shard_map/reduce_scatter | solution.py:227
  476.9 7.1 copy-start.21
  493.9 208.3 %reduce-scatter.9.cloned.1.call-start = ((), (), s32[]{:S(2)}) async-start(), calls=%async_computation.9 | async-start | bytes 7864320 | tf_op jit(solution)/shard_map/reduce_scatter | solution.py:270
  501.0 140.3 %copy-start.51 = (bf16[768]{0:T(1024)(128)(2,1)S(1)}, bf16[768]{0:T(1024)(128)(2,1)}, u32[]{:S(2)}) copy-start(bf16[768]{0:T(1024)(128)(2,1)} %param.30) | copy-start | bytes 4612
  501.0 339.6 %all-reduce.4.cloned.1.call-start = ((), (), s32[]{:S(2)}) async-start(), calls=%async_computation.16 | async-start | bytes 7077888 | tf_op jit(solution)/shard_map/psum | solution.py:283
  648.2 8.4 copy-start.17
  648.2 54.0 %copy-start.8 = (bf16[512,768]{1,0:T(8,128)(2,1)S(1)}, bf16[512,768]{1,0:T(8,128)(2,1)}, u32[]{:S(2)}) copy-start(bf16[512,768]{1,0:T(8,128)(2,1)} %param.18) | copy-start | bytes 2359300
  648.2 53.9 %copy-start.34 = (f32[768]{0:T(1024)S(1)}, f32[768]{0:T(1024)}, u32[]{:S(2)}) copy-start(f32[768]{0:T(1024)} %copy-done.33) | copy-start | bytes 9220
  648.2 53.9 %copy-start.36 = (f32[512]{0:T(512)S(1)}, f32[512]{0:T(512)}, u32[]{:S(2)}) copy-start(f32[512]{0:T(512)} %copy-done.35) | copy-start | bytes 6148
  656.6 47.5 %copy-start.42 = (f32[512]{0:T(512)S(1)}, f32[512]{0:T(512)}, u32[]{:S(2)}) copy-start(f32[512]{0:T(512)} %copy-done.41) | copy-start | bytes 6148
  656.6 47.6 %copy-start.38 = (f32[512]{0:T(512)S(1)}, f32[512]{0:T(512)}, u32[]{:S(2)}) copy-start(f32[512]{0:T(512)} %copy-done.37) | copy-start | bytes 6148
  656.6 48.4 %copy-start.14 = (f32[512,768]{1,0:T(8,128)S(1)}, f32[512,768]{1,0:T(8,128)}, u32[]{:S(2)}) copy-start(f32[512,768]{1,0:T(8,128)} %copy-done.13) | copy-start | bytes 4718596
  656.6 48.4 %copy-start.40 = (f32[512]{0:T(512)S(1)}, f32[512]{0:T(512)}, u32[]{:S(2)}) copy-start(f32[512]{0:T(512)} %copy-done.39) | copy-start | bytes 6148
  (57 other events, 240.5 us)
Sparse Core Ops, SparseCore 0:
  14.6 31.2 all-gather.8
  47.8 38.9 all-gather.12
  150.5 58.0 reduce-scatter.6
  210.5 38.8 all-gather.14
  269.9 28.5 all-gather.10
  302.1 15.2 reduce-scatter.12
  452.1 28.2 reduce-scatter.10
  484.3 76.4 reduce-scatter.14
  564.7 76.4 reduce-scatter.16
  643.8 58.3 reduce-scatter.8
  704.8 135.7 all-reduce.3
where the time goes:
time: 863 us; the launch traced here: 854 us
  waiting for transfers between devices  381 us (44%)
  matrix products  218 us (25%)
  other arithmetic  75.6 us (9%)
  blocking collectives  72.2 us (8%)
  local copies, waits for them, and re-layouts  71.5 us (8%)
  loops' own time  19.4 us (2%)
  between operations  15.1 us (2%)
    psum x1, waiting for transfers between devices, body(): lax.psum((qkv_block_grad, out_block_grad, fc_block_grad, proj_block_grad)...  88.2 us
    reduce_scatter x1, waiting for transfers between devices, body(): lax.psum_scatter(proj_grid_grad.reshape(row_count * col_count, hidden_col...  80.4 us
    reduce_scatter x1, waiting for transfers between devices, body(): lax.psum_scatter(fc_grid_grad.reshape(row_count * col_count, -1, hidden_c...  59.7 us
    reduce_scatter x1, waiting for transfers between devices, body(): lax.psum_scatter(jnp.einsum('tje,dje->td', qkv_grad, qkv_full, preferred_...  45.1 us
    psum x1, blocking collectives, body(): lax.psum((vector_grads, qv_grad_wide, fc_bias_grad), ('dp', 'row', 'col'))  43.7 us
    reduce_scatter x1, waiting for transfers between devices, body(): lax.psum_scatter(jnp.dot(context, out_full, preferred_element_type=jnp.fl...  36.3 us
    dot_general x8, matrix products, masked_scores(): jnp.einsum('qhd,khd->hqk', query_block, keys_seq, preferred_element_type=...  36.1 us
    all_gather x1, waiting for transfers between devices, body(): lax.all_gather(proj_weight[None], ('row', 'col'), axis=0, tiled=True)  30.4 us
  transfers between devices with their start and end apart: 11, of which 8 were waited for; matrix products, arithmetic and copies ran while one was open for 38% of the time, Pallas kernels for 0%

commit v1 on v0

v1 whole, which is shorter than its diff:
```python
import functools
import jax
import jax.numpy as jnp
from jax import lax
from jax.experimental import pallas as pl
from jax.experimental.pallas import tpu as pltpu
from jax.sharding import PartitionSpec as P

HEAD_DIM = 64
masked_score = -1e30


def tile_start(tile, tile_rows, block_rows, here):
    per_block = block_rows // tile_rows
    return pl.multiple_of(
        (here ^ (tile // per_block)) * block_rows + tile % per_block * tile_rows, tile_rows
    )


def forward_kernel(here_ref, q_ref, k_ref, v_ref, low_ref, wide_ref, lse_ref, keys, *, block, tq, tk):
    here = here_ref[0]
    seq = q_ref.shape[1]
    keys[...] = k_ref[...].T
    for qi in range(seq // tq):
        q_at = tile_start(qi, tq, block, here)
        query = q_ref[:, pl.ds(q_at, tq)] * 0.125
        peak = total = acc = None
        for ki in range((qi + 1) * tq // tk if tq >= tk else qi * tq // tk + 1):
            k_at = tile_start(ki, tk, block, here)
            scores = jnp.dot(keys[pl.ds(k_at, tk), :], query, preferred_element_type=jnp.float32)
            if (ki + 1) * tk > qi * tq + 1:
                k_pos = ki * tk + lax.broadcasted_iota(jnp.int32, (tk, tq), 0)
                q_pos = qi * tq + lax.broadcasted_iota(jnp.int32, (tk, tq), 1)
                scores = jnp.where(k_pos <= q_pos, scores, masked_score)
            tile_peak = jnp.max(scores, axis=0, keepdims=True)
            new_peak = tile_peak if peak is None else jnp.maximum(peak, tile_peak)
            shifted = jnp.exp(scores - new_peak)
            tile_total = jnp.sum(shifted, axis=0, keepdims=True)
            part = jnp.dot(
                v_ref[:, pl.ds(k_at, tk)], shifted.astype(jnp.bfloat16),
                preferred_element_type=jnp.float32,
            )
            if peak is None:
                total, acc = tile_total, part
            else:
                shrink = jnp.exp(peak - new_peak)
                total = total * shrink + tile_total
                acc = acc * shrink + part
            peak = new_peak
        wide = acc / total
        wide_ref[:, pl.ds(q_at, tq)] = wide
        low_ref[:, pl.ds(q_at, tq)] = wide.astype(jnp.bfloat16)
        lse_ref[0, :, pl.ds(q_at, tq)] = peak + jnp.log(total)


def backward_kernel(
    here_ref, q_ref, k_ref, v_ref, g_ref, wide_ref, lse_ref, dq_ref, dk_ref, dv_ref,
    keys, values, queries, grads, dkeys, dvalues, *, block, tq, tk,
):
    here = here_ref[0]
    seq = q_ref.shape[1]
    keys[...] = k_ref[...].T
    values[...] = v_ref[...].T
    queries[...] = (q_ref[...] * 0.125).T
    grads[...] = g_ref[...].T
    for qi in range(seq // tq):
        q_at = tile_start(qi, tq, block, here)
        query = q_ref[:, pl.ds(q_at, tq)] * 0.125
        grad = g_ref[:, pl.ds(q_at, tq)]
        query_rows = queries[pl.ds(q_at, tq), :]
        grad_rows = grads[pl.ds(q_at, tq), :]
        lse = lse_ref[0, :, pl.ds(q_at, tq)]
        inner = jnp.sum(
            grad.astype(jnp.float32) * wide_ref[:, pl.ds(q_at, tq)], axis=0, keepdims=True
        )
        acc = None
        for ki in range((qi + 1) * tq // tk if tq >= tk else qi * tq // tk + 1):
            k_at = tile_start(ki, tk, block, here)
            k_rows = pl.ds(k_at, tk)
            scores = jnp.dot(keys[k_rows, :], query, preferred_element_type=jnp.float32)
            probs = jnp.exp(scores - lse)
            if (ki + 1) * tk > qi * tq + 1:
                k_pos = ki * tk + lax.broadcasted_iota(jnp.int32, (tk, tq), 0)
                q_pos = qi * tq + lax.broadcasted_iota(jnp.int32, (tk, tq), 1)
                probs = jnp.where(k_pos <= q_pos, probs, 0.0)
            prob_grad = jnp.dot(values[k_rows, :], grad, preferred_element_type=jnp.float32)
            score_grad = (probs * (prob_grad - inner)).astype(jnp.bfloat16)
            dv = jnp.dot(probs.astype(jnp.bfloat16), grad_rows, preferred_element_type=jnp.float32)
            dk = jnp.dot(score_grad, query_rows, preferred_element_type=jnp.float32)
            dq = jnp.dot(
                k_ref[:, k_rows], score_grad, preferred_element_type=jnp.float32
            )
            acc = dq if acc is None else acc + dq
            if qi * tq // tk * tk <= ki * tk and qi * tq % tk == 0:
                dkeys[k_rows, :] = dk
                dvalues[k_rows, :] = dv
            else:
                dkeys[k_rows, :] += dk
                dvalues[k_rows, :] += dv
        dq_ref[:, pl.ds(q_at, tq)] = (acc * 0.125).astype(jnp.bfloat16)
    dk_ref[...] = dkeys[...].T.astype(jnp.bfloat16)
    dv_ref[...] = dvalues[...].T.astype(jnp.bfloat16)


def attend_forward(here, qkv, block, tq=512, tk=512):
    feats, seq = qkv.shape
    heads = feats // 3 // HEAD_DIM
    part = lambda j: pl.BlockSpec((HEAD_DIM, seq), lambda h, _: (j * heads + h, 0))
    return pl.pallas_call(
        functools.partial(forward_kernel, block=block, tq=tq, tk=tk),
        out_shape=(
            jax.ShapeDtypeStruct((feats // 3, seq), jnp.bfloat16),
            jax.ShapeDtypeStruct((feats // 3, seq), jnp.float32),
            jax.ShapeDtypeStruct((heads, 1, seq), jnp.float32),
        ),
        grid_spec=pltpu.PrefetchScalarGridSpec(
            num_scalar_prefetch=1,
            grid=(heads,),
            in_specs=[part(0), part(1), part(2)],
            out_specs=(part(0), part(0), pl.BlockSpec((1, 1, seq), lambda h, _: (h, 0, 0))),
            scratch_shapes=[pltpu.VMEM((seq, HEAD_DIM), jnp.bfloat16)],
        ),
        compiler_params=pltpu.CompilerParams(vmem_limit_bytes=48 * 2**20),
        cost_estimate=pl.CostEstimate(
            flops=heads * seq * seq * 512, bytes_accessed=feats * seq * 5,
            transcendentals=heads * seq * seq // 2,
        ),
        name="attn_forward",
    )(here, qkv, qkv, qkv)


def attend_backward(here, qkv, grad, wide, lse, block, tq=512, tk=512, first=0, count=None):
    feats, seq = qkv.shape
    heads = feats // 3 // HEAD_DIM
    count = heads if count is None else count
    part = lambda j: pl.BlockSpec((HEAD_DIM, seq), lambda h, _: (j * heads + first + h, 0))
    done = pl.BlockSpec((HEAD_DIM, seq), lambda h, _: (h, 0))
    return pl.pallas_call(
        functools.partial(backward_kernel, block=block, tq=tq, tk=tk),
        out_shape=(jax.ShapeDtypeStruct((count * HEAD_DIM, seq), jnp.bfloat16),) * 3,
        grid_spec=pltpu.PrefetchScalarGridSpec(
            num_scalar_prefetch=1,
            grid=(count,),
            in_specs=[
                part(0), part(1), part(2), part(0), part(0),
                pl.BlockSpec((1, 1, seq), lambda h, _: (first + h, 0, 0)),
            ],
            out_specs=(done, done, done),
            scratch_shapes=[pltpu.VMEM((seq, HEAD_DIM), jnp.bfloat16)] * 4
            + [pltpu.VMEM((seq, HEAD_DIM), jnp.float32)] * 2,
        ),
        compiler_params=pltpu.CompilerParams(vmem_limit_bytes=48 * 2**20),
        cost_estimate=pl.CostEstimate(
            flops=count * seq * seq * 1280, bytes_accessed=count * seq * 64 * 18,
            transcendentals=count * seq * seq // 2,
        ),
        name="attn_backward",
    )(here, qkv, qkv, qkv, grad, wide, lse)


eps = 1e-05


def layer_norm(rows, gain, shift):
    average = jnp.mean(rows, axis=-1, keepdims=True)
    centred = rows - average
    variance = jnp.mean(centred * centred, axis=-1, keepdims=True)
    return centred * lax.rsqrt(variance + eps) * gain + shift


def gelu_tanh(values):
    return jax.nn.gelu(values, approximate=True)


def swap(value, axis, step):
    count = lax.axis_size(axis)
    return lax.ppermute(value, axis, [(i, i ^ step) for i in range(count)])


def gather_xor(value, axis):
    count = lax.axis_size(axis)
    held = {0: value}
    step = count // 2
    while step:
        held.update({r ^ step: swap(held[r], axis, step) for r in list(held)})
        step //= 2
    return [held[r] for r in range(count)]


def gather_row(value):
    index = lax.axis_index("row")
    parts = gather_xor(value, "row")
    if len(parts) == 2:
        return jnp.where(index == 0, jnp.stack(parts), jnp.stack(parts[::-1]))
    stacked = jnp.zeros((len(parts),) + value.shape, value.dtype)
    for step, part in enumerate(parts):
        stacked = lax.dynamic_update_index_in_dim(stacked, part, index ^ step, 0)
    return stacked


def scatter_row(stacked):
    index = lax.axis_index("row")
    total = lax.dynamic_index_in_dim(stacked, index, 0, keepdims=False).astype(jnp.float32)
    for step in range(1, stacked.shape[0]):
        part = lax.dynamic_index_in_dim(stacked, index ^ step, 0, keepdims=False)
        total = total + swap(part.astype(jnp.bfloat16), "row", step).astype(jnp.float32)
    return total


def sum_dp(block):
    count = lax.axis_size("dp")
    index = lax.axis_index("dp")
    pieces = block.reshape((count, block.shape[0] // count) + block.shape[1:])
    total = lax.dynamic_index_in_dim(pieces, index, 0, keepdims=False).astype(jnp.float32)
    for step in range(1, count):
        part = lax.dynamic_index_in_dim(pieces, index ^ step, 0, keepdims=False)
        total = total + swap(part.astype(jnp.bfloat16), "dp", step).astype(jnp.float32)
    total = total.astype(jnp.bfloat16)
    out = jnp.zeros(pieces.shape, jnp.float32)
    for step in range(count):
        part = total if step == 0 else swap(total, "dp", step)
        out = lax.dynamic_update_index_in_dim(out, part.astype(jnp.float32), index ^ step, 0)
    return out.reshape(block.shape)


def sum_small(value, axes):
    for axis in axes:
        step = 1
        while step < lax.axis_size(axis):
            value = value + swap(value, axis, step)
            step *= 2
    return value


def contract(left, right, left_dim, right_dim):
    return lax.dot_general(
        left, right, (((left_dim,), (right_dim,)), ((), ())), preferred_element_type=jnp.float32
    )


def scatter_col(near, far, rows):
    blocks = [near[:rows], near[rows:], far[:rows], far[rows:]]
    away = blocks[2].astype(jnp.float32) + swap(blocks[3], "col", 1).astype(jnp.float32)
    away = swap(away.astype(jnp.bfloat16), "col", 2).astype(jnp.float32)
    return blocks[0].astype(jnp.float32) + swap(blocks[1], "col", 1).astype(jnp.float32) + away


def body(
    inputs,
    pre_attn_gain,
    pre_attn_shift,
    qkv_weight,
    qv_bias,
    out_weight,
    out_bias,
    pre_mlp_gain,
    pre_mlp_shift,
    fc_weight,
    fc_bias,
    proj_weight,
    proj_bias,
    cotangent,
):
    low = jnp.bfloat16
    wide = jnp.float32
    rows, width = inputs.shape
    cols = lax.axis_size("col")
    row_count = lax.axis_size("row")
    row_index = lax.axis_index("row")
    here = lax.axis_index("col").astype(jnp.int32).reshape(1)
    head_cols = qkv_weight.shape[2]
    hidden_cols = fc_weight.shape[1]
    every = ("col", "row", "dp")
    gain_one, shift_one = pre_attn_gain.astype(wide), pre_attn_shift.astype(wide)
    gain_two, shift_two = pre_mlp_gain.astype(wide), pre_mlp_shift.astype(wide)

    stream = inputs.astype(wide)
    normed_one = layer_norm(stream, gain_one, shift_one).astype(low)
    normed = gather_xor(normed_one, "col")
    normed_near = jnp.concatenate(normed[:2], 0)
    normed_far = jnp.concatenate(normed[2:], 0)
    qkv_full = gather_row(qkv_weight.reshape(-1, 3 * head_cols)).reshape(width, 3 * head_cols)
    bias_wide = qv_bias.astype(wide)
    bias_col = jnp.concatenate([bias_wide[0], jnp.zeros_like(bias_wide[0]), bias_wide[1]])[:, None]
    qkv = jnp.concatenate(
        [
            (contract(qkv_full, part, 0, 1) + bias_col).astype(low)
            for part in (normed_near, normed_far)
        ],
        1,
    )
    context, context_wide, lse = attend_forward(here, qkv, rows)
    out_rows = jnp.moveaxis(gather_row(out_weight), 0, 1).reshape(head_cols, width)
    out_full = jnp.concatenate(gather_xor(out_rows, "col"), 0)
    context_own = jnp.concatenate(
        [
            context[:, :rows] if r == 0 else swap(context[:, r * rows : (r + 1) * rows], "col", r)
            for r in range(cols)
        ],
        0,
    )
    mid_stream = stream + contract(context_own, out_full, 0, 0) + out_bias.astype(wide)
    normed_two = layer_norm(mid_stream, gain_two, shift_two).astype(low)

    fc_full = gather_row(fc_weight).reshape(width, hidden_cols)
    proj_full = jnp.moveaxis(gather_row(proj_weight), 0, 1).reshape(hidden_cols, width)
    fc_bias_wide = fc_bias.astype(wide)
    cot = gather_xor(cotangent, "col")
    two = gather_xor(normed_two, "col")
    sides = []
    for first in (0, 2):
        normed_side = jnp.concatenate(two[first : first + 2], 0)
        cot_side = jnp.concatenate(cot[first : first + 2], 0)
        pre_act = contract(normed_side, fc_full, 1, 0) + fc_bias_wide
        hidden_wide, gelu_pull = jax.vjp(gelu_tanh, pre_act)
        hidden = hidden_wide.astype(low)
        pre_grad = gelu_pull(contract(cot_side, proj_full, 1, 1))[0].astype(low)
        two_grad = contract(pre_grad, fc_full, 1, 1).astype(low)
        mlp_out = contract(hidden, proj_full, 1, 0).astype(low)
        fc_grad = contract(normed_side, pre_grad, 0, 0)
        proj_grad = contract(cot_side, hidden, 0, 0)
        sides.append(
            (two_grad, mlp_out, fc_grad, proj_grad, jnp.sum(pre_grad, axis=0, dtype=wide))
        )
    near, far = sides
    normed_two_grad = scatter_col(near[0], far[0], rows)
    out_grad = cotangent.astype(wide)
    norm_two_pull = jax.vjp(layer_norm, mid_stream, gain_two, shift_two)[1]
    stream_two, gain_two_grad, shift_two_grad = norm_two_pull(normed_two_grad)
    mid_grad = out_grad + stream_two
    mid_low = mid_grad.astype(low)
    context_grad_own = contract(out_full, mid_low, 1, 1).astype(low)
    context_grad = jnp.concatenate(
        [
            context_grad_own[:head_cols]
            if r == 0
            else swap(context_grad_own[r * head_cols : (r + 1) * head_cols], "col", r)
            for r in range(cols)
        ],
        1,
    )
    mlp_sum = scatter_col(near[1], far[1], rows)
    block_out = (mid_stream + mlp_sum + proj_bias.astype(wide)).astype(low)
    fc_sum = sum_dp(scatter_row((near[2] + far[2]).reshape(row_count, -1, hidden_cols)))
    proj_sum = sum_dp(scatter_row((near[3] + far[3]).reshape(row_count, -1, hidden_cols))).T
    out_part = contract(context_own, mid_low, 1, 0)
    out_block = out_part[:head_cols]
    for r in range(1, cols):
        part = out_part[r * head_cols : (r + 1) * head_cols].astype(low)
        out_block = out_block + swap(part, "col", r).astype(wide)
    out_block = jnp.moveaxis(out_block.reshape(head_cols, row_count, -1), 1, 0)
    out_sum = sum_dp(scatter_row(out_block))
    early = jnp.stack(
        [
            jnp.sum(mid_low, axis=0, dtype=wide),
            gain_two_grad,
            shift_two_grad,
            jnp.sum(out_grad, axis=0),
        ]
    )
    early_sum = sum_small(early, every)
    fc_bias_sum = sum_small((near[4] + far[4]).reshape(1, -1), ("row", "dp"))[0]

    grads = attend_backward(here, qkv, context_grad, context_wide, lse, rows)
    qkv_grad = jnp.concatenate(grads, 0)
    qv_part = jnp.stack(
        [jnp.sum(grads[0], axis=1, dtype=wide), jnp.sum(grads[2], axis=1, dtype=wide)]
    )
    qv_sum = sum_small(qv_part, ("row", "dp"))
    weights = gather_xor(qkv_full, "col")
    normed_one_grad = 0.0
    for r in range(cols):
        part = qkv_grad[:, r * rows : (r + 1) * rows]
        part = part if r == 0 else swap(part, "col", r)
        normed_one_grad = normed_one_grad + contract(part, weights[r], 0, 1)
    qkv_part = contract(normed_near, qkv_grad[:, : 2 * rows], 0, 1)
    qkv_part = qkv_part + contract(normed_far, qkv_grad[:, 2 * rows :], 0, 1)
    qkv_sum = sum_dp(scatter_row(qkv_part.reshape(row_count, -1, 3 * head_cols)))
    norm_one_pull = jax.vjp(layer_norm, stream, gain_one, shift_one)[1]
    stream_one, gain_one_grad, shift_one_grad = norm_one_pull(normed_one_grad)
    input_grad = (mid_grad + stream_one).astype(low)
    late_sum = sum_small(jnp.stack([gain_one_grad, shift_one_grad]), every)
    return (
        block_out,
        input_grad,
        late_sum[0],
        late_sum[1],
        qkv_sum.reshape(qkv_weight.shape),
        qv_sum,
        out_sum,
        early_sum[0],
        early_sum[1],
        early_sum[2],
        fc_sum,
        fc_bias_sum,
        proj_sum,
        early_sum[3],
    )


def solution(mesh):
    placed = (
        P(("dp", "row", "col"), None),
        P(),
        P(),
        P("row", None, "col"),
        P(None, "col"),
        P("col", "row"),
        P(),
        P(),
        P(),
        P("row", "col"),
        P("col"),
        P("col", "row"),
        P(),
        P(("dp", "row", "col"), None),
    )
    return jax.shard_map(
        body,
        mesh=mesh,
        in_specs=placed,
        out_specs=(
            P(("dp", "row", "col"), None),
            P(("dp", "row", "col"), None),
            P(),
            P(),
            P("row", None, "col"),
            P(None, "col"),
            P("col", "row"),
            P(),
            P(),
            P(),
            P("row", "col"),
            P("col"),
            P("col", "row"),
            P(),
        ),
        check_vma=False,
    )
```

time: 863 us -> 389 us (0.45)
  waiting for transfers between devices: 381 us -> 123 us
  matrix products: 218 us -> 46.1 us
  starting transfers between devices: 0.45 us -> 75.1 us
  blocking collectives: 72.2 us -> 0 us
  Pallas kernels: 0 us -> 36.2 us
  other arithmetic: 75.6 us -> 40.2 us
  loops' own time: 19.4 us -> 0 us
  between operations: 15.1 us -> 2.26 us
  local copies, waits for them, and re-layouts: 71.5 us -> 59.2 us
    reduce_scatter x6 -> x0, waiting for transfers between devices: 222 us -> none  [the longest x1 80.4 us: body(): lax.psum_scatter(proj_grid_grad.reshape(row_count * col_count, hidden_col...]
    dot_general x38 -> x23, matrix products: 211 us -> 46.1 us  [contract(): lax.dot_general(left, right, (((left_dim,), (right_dim,)), ((), ())), pre...]
    ppermute x0 -> x81, waiting for transfers between devices: none -> 123 us  [swap(): return lax.ppermute(value, axis, [(i, i ^ step) for i in range(count)])]
    psum x1 -> x0, waiting for transfers between devices: 88.2 us -> none  [body(): lax.psum((qkv_block_grad, out_block_grad, fc_block_grad, proj_block_grad)...]
    ppermute x0 -> x81, starting transfers between devices: none -> 75.1 us  [swap(): return lax.ppermute(value, axis, [(i, i ^ step) for i in range(count)])]
    all_gather x4 -> x0, waiting for transfers between devices: 69.9 us -> none  [the longest x1 30.4 us: body(): lax.all_gather(proj_weight[None], ('row', 'col'), axis=0, tiled=True)]
    psum x1 -> x0, blocking collectives: 43.7 us -> none  [body(): lax.psum((vector_grads, qv_grad_wide, fc_bias_grad), ('dp', 'row', 'col'))]
    pallas_call x0 -> x2, Pallas kernels: none -> 36.2 us  [the longest x1 22.5 us: attend_backward(): pl.pallas_call(functools.partial(backward_kernel, block=block, tq=tq, tk=...]
  transfers between devices with their start and end apart: 11 -> 81, of which waited for: 8 -> 30; matrix products, arithmetic and copies ran while one was open for 38% -> 29% of each run, Pallas kernels for 0% -> 9%
where the time goes in v1:
time: 389 us; the launch traced here: 382 us
  waiting for transfers between devices  123 us (32%)
  starting transfers between devices  75.1 us (19%)
  local copies, waits for them, and re-layouts  59.2 us (15%)
  matrix products  46.1 us (12%)
  other arithmetic  40.2 us (10%)
  Pallas kernels  36.2 us (9%)
    ppermute x81, waiting for transfers between devices, swap(): return lax.ppermute(value, axis, [(i, i ^ step) for i in range(count)])  123 us
    ppermute x81, starting transfers between devices, swap(): return lax.ppermute(value, axis, [(i, i ^ step) for i in range(count)])  75.1 us
    dot_general x23, matrix products, contract(): lax.dot_general(left, right, (((left_dim,), (right_dim,)), ((), ())), pre...  46.1 us
    dynamic_update_slice x4, local copies, waits for them, and re-layouts, sum_dp(): lax.dynamic_update_index_in_dim(out, part.astype(jnp.float32), index ^ st...  27.5 us
    pallas_call x1, Pallas kernels, attend_backward(): pl.pallas_call(functools.partial(backward_kernel, block=block, tq=tq, tk=...  22.5 us
    pallas_call x1, Pallas kernels, attend_forward(): pl.pallas_call(functools.partial(forward_kernel, block=block, tq=tq, tk=t...  13.7 us
    unnamed x101, local copies, waits for them, and re-layouts  10.1 us
  transfers between devices with their start and end apart: 81, of which 30 were waited for; matrix products, arithmetic and copies ran while one was open for 29% of the time, Pallas kernels for 9%

profile of v1, /device:TPU:0, one launch (start us, length us, event | category | flops | bytes accessed | tf_op | source)
XLA Modules:
  0.0 382.0 jit_solution(15971217716586252190)
XLA Ops:
  4.0 3.0 collective-permute-start.2
  11.8 11.2 %collective-permute-done.7 = bf16[192,384]{1,0:T(8,128)(2,1)S(1)} collective-permute-done((bf16[192,384]{1,0:T(8,128)(2,1)S(1)}, bf16[192,384]{1,0:T(8,128)(2,1)S(1)}, u32[]{:S(2)}, u32[]{:S(2)}) %collective-permute-start.7) | collective-permute-done | bytes 147488 | tf_op jit(solution)/shard_map/ppermute | solution.py:177
  42.3 13.7 %attn_forward.1 = (bf16[192,2048]{1,0:T(8,128)(2,1)S(1)}, f32[192,2048]{1,0:T(8,128)S(1)}, f32[3,1,2048]{2,1,0:T(1,128)S(1)}) custom-call(s32[1]{0:T(128)} %bitcast.here_ref, bf16[576,2048]{1,0:T(8,128)(2,1)S(1)} %pad_maximum_fusion.q_ref.k_ref.v_ref, bf16[576,2048]{1,0:T(8,128)(2,1)S(1)} %pad_maximum_fusion.q_ref.k_ref.v_ref, ...), custom_call_target="tpu_custom_call" | custom-call | flops 6442450944 | bytes 5898240 | tf_op jit(solution)/shard_map/attn_forward/pallas_call | solution.py:109
  59.6 4.7 %collective-permute-done.5 = bf16[192,512]{1,0:T(8,128)(2,1)S(1)} collective-permute-done((bf16[192,512]{1,0:T(8,128)(2,1)S(1)}, bf16[192,512]{1,0:T(8,128)(2,1)S(1)}, u32[]{:S(2)}, u32[]{:S(2)}) %collective-permute-start.5) | collective-permute-done | bytes 196640 | tf_op jit(solution)/shard_map/ppermute | solution.py:177
  64.2 2.7 collective-permute-done.6
  70.1 4.4 %collective-permute-done.13 = bf16[768,384]{0,1:T(8,128)(2,1)S(1)} collective-permute-done((bf16[768,384]{0,1:T(8,128)(2,1)}, bf16[768,384]{0,1:T(8,128)(2,1)S(1)}, u32[]{:S(2)}, u32[]{:S(2)}) %collective-permute-start.13) | collective-permute-done | bytes 589856 | tf_op jit(solution)/shard_map/ppermute | solution.py:177
  77.8 11.6 %collective-permute-done.15 = bf16[512,768]{1,0:T(8,128)(2,1)S(1)} collective-permute-done((bf16[512,768]{1,0:T(8,128)(2,1)S(1)}, bf16[512,768]{1,0:T(8,128)(2,1)S(1)}, u32[]{:S(2)}, u32[]{:S(2)}) %collective-permute-start.15) | collective-permute-done | bytes 786464 | tf_op jit(solution)/shard_map/ppermute | solution.py:177
  102.3 6.3 %convert_reduce_fusion.1 = (f32[768]{0:T(1024)S(1)}, bf16[1024,768]{1,0:T(8,128)(2,1)S(1)}, f32[768]{0:T(1024)S(1)}, bf16[1024,768]{1,0:T(8,128)(2,1)S(1)}) fusion(f32[1024,768]{1,0:T(8,128)S(1)} %fusion.97, f32[1024,768]{1,0:T(8,128)S(1)} %fusion.30, f32[768]{0:T(1024)S(1)} %copy-done.31, f32[1024,768]{1,0:T(8,128)S(1)} %fusion.96, ...), kind=kOutput, calls=%fused_computation.19 | convolution fusion | flops 1244133888 | bytes 15344640 | tf_op jit(solution)/shard_map/dot_general | solution.py:236
  114.5 3.0 collective-permute-done.71
  121.1 2.6 collective-permute-start.73
  130.6 3.3 collective-permute-done.64
  137.3 6.8 %collective-permute-done.76 = bf16[96,768]{1,0:T(8,128)(2,1)S(1)} collective-permute-done((bf16[96,768]{1,0:T(8,128)(2,1)S(1)}, bf16[96,768]{1,0:T(8,128)(2,1)S(1)}, u32[]{:S(2)}, u32[]{:S(2)}) %collective-permute-start.76) | collective-permute-done | bytes 147488 | tf_op jit(solution)/shard_map/ppermute | solution.py:177
  147.2 8.0 %collective-permute-done.66 = bf16[96,768]{1,0:T(8,128)(2,1)S(1)} collective-permute-done((bf16[96,768]{1,0:T(8,128)(2,1)S(1)}, bf16[96,768]{1,0:T(8,128)(2,1)S(1)}, u32[]{:S(2)}, u32[]{:S(2)}) %collective-permute-start.66) | collective-permute-done | bytes 147488 | tf_op jit(solution)/shard_map/ppermute | solution.py:177
  165.6 8.3 %collective-permute-done.79 = bf16[96,768]{1,0:T(8,128)(2,1)S(1)} collective-permute-done((bf16[96,768]{1,0:T(8,128)(2,1)S(1)}, bf16[96,768]{1,0:T(8,128)(2,1)S(1)}, u32[]{:S(2)}, u32[]{:S(2)}) %collective-permute-start.79) | collective-permute-done | bytes 147488 | tf_op jit(solution)/shard_map/ppermute | solution.py:177
  175.9 2.7 copy.73
  182.4 5.9 %collective-permute-done.69 = bf16[96,768]{1,0:T(8,128)(2,1)S(1)} collective-permute-done((bf16[96,768]{1,0:T(8,128)(2,1)}, bf16[96,768]{1,0:T(8,128)(2,1)S(1)}, u32[]{:S(2)}, u32[]{:S(2)}) %collective-permute-start.69) | collective-permute-done | bytes 147488 | tf_op jit(solution)/shard_map/ppermute | solution.py:177
  190.9 4.6 %collective-permute-done.70 = bf16[96,768]{1,0:T(8,128)(2,1)S(1)} collective-permute-done((bf16[96,768]{1,0:T(8,128)(2,1)}, bf16[96,768]{1,0:T(8,128)(2,1)S(1)}, u32[]{:S(2)}, u32[]{:S(2)}) %collective-permute-start.70) | collective-permute-done | bytes 147488 | tf_op jit(solution)/shard_map/ppermute | solution.py:177
  198.1 2.7 multiply_reduce_fusion
  200.8 11.0 %collective-permute-done.18 = bf16[512,768]{1,0:T(8,128)(2,1)S(1)} collective-permute-done((bf16[512,768]{1,0:T(8,128)(2,1)}, bf16[512,768]{1,0:T(8,128)(2,1)S(1)}, u32[]{:S(2)}, u32[]{:S(2)}) %collective-permute-start.18) | collective-permute-done | bytes 786464 | tf_op jit(solution)/shard_map/ppermute | solution.py:177
  211.8 3.6 fusion.88
  231.5 22.5 %attn_backward.1 = (bf16[192,2048]{1,0:T(8,128)(2,1)S(1)}, bf16[192,2048]{1,0:T(8,128)(2,1)S(1)}, bf16[192,2048]{1,0:T(8,128)(2,1)S(1)}) custom-call(s32[1]{0:T(128)} %bitcast.here_ref, bf16[576,2048]{1,0:T(8,128)(2,1)} %copy-done, bf16[576,2048]{1,0:T(8,128)(2,1)} %copy-done, bf16[576,2048]{1,0:T(8,128)(2,1)} %copy-done, ...), custom_call_target="tpu_custom_call" | custom-call | flops 16106127360 | bytes 7077888 | tf_op jit(solution)/shard_map/attn_backward/pallas_call | solution.py:138
  265.0 3.0 fusion.37
  280.5 3.3 collective-permute-start.54
  285.8 3.8 %collective-permute-done.55 = bf16[48,384]{1,0:T(8,128)(2,1)S(1)} collective-permute-done((bf16[48,384]{1,0:T(8,128)(2,1)S(1)}, bf16[48,384]{1,0:T(8,128)(2,1)S(1)}, u32[]{:S(2)}, u32[]{:S(2)}) %collective-permute-start.55) | collective-permute-done | bytes 36896 | tf_op jit(solution)/shard_map/ppermute | solution.py:177
  294.4 4.6 %collective-permute-done.57 = bf16[48,384]{1,0:T(8,128)(2,1)S(1)} collective-permute-done((bf16[48,384]{1,0:T(8,128)(2,1)S(1)}, bf16[48,384]{1,0:T(8,128)(2,1)S(1)}, u32[]{:S(2)}, u32[]{:S(2)}) %collective-permute-start.57) | collective-permute-done | bytes 36896 | tf_op jit(solution)/shard_map/ppermute | solution.py:177
  308.3 7.3 %collective-permute-done.32 = bf16[576,512]{1,0:T(8,128)(2,1)S(1)} collective-permute-done((bf16[576,512]{1,0:T(8,128)(2,1)}, bf16[576,512]{1,0:T(8,128)(2,1)S(1)}, u32[]{:S(2)}, u32[]{:S(2)}) %collective-permute-start.32) | collective-permute-done | bytes 589856 | tf_op jit(solution)/shard_map/ppermute | solution.py:177
  319.4 2.9 convert_reduce_fusion.3
  346.8 7.1 %dynamic_update_slice.51 = f32[4,96,576]{1,0,2:T(4,128)S(1)} dynamic-update-slice(f32[4,96,576]{1,0,2:T(4,128)S(1)} %broadcast_in_dim.144, f32[1,96,576]{1,0,2:T(1,128)S(1)} %copy.68, s32[]{:T(128)S(6)} %select_n.113, s32[]{:T(128)} %constant.137.clone.1, s32[]{:T(128)} %constant.137.clone.1) | dynamic-update-slice | bytes 442372 | tf_op jit(solution)/shard_map/jit(dynamic_update_index_in_dim)/dynamic_update_slice | solution.py:222
  355.6 3.0 collective-permute-done.63
  359.8 6.8 %dynamic_update_slice.52 = f32[4,96,576]{1,0,2:T(4,128)S(1)} dynamic-update-slice(f32[4,96,576]{1,0,2:T(4,128)S(1)} %dynamic_update_slice.51, f32[1,96,576]{1,0,2:T(1,128)S(1)} %copy.69, s32[]{:T(128)S(6)} %select_n.114, s32[]{:T(128)} %constant.137.clone.1, s32[]{:T(128)} %constant.137.clone.1) | dynamic-update-slice | bytes 442372 | tf_op jit(solution)/shard_map/jit(dynamic_update_index_in_dim)/dynamic_update_slice | solution.py:222
  366.6 6.8 %dynamic_update_slice.53 = f32[4,96,576]{1,0,2:T(4,128)S(1)} dynamic-update-slice(f32[4,96,576]{1,0,2:T(4,128)S(1)} %dynamic_update_slice.52, f32[1,96,576]{1,0,2:T(1,128)S(1)} %copy.70, s32[]{:T(128)S(6)} %select_n.115, s32[]{:T(128)} %constant.137.clone.1, s32[]{:T(128)} %constant.137.clone.1) | dynamic-update-slice | bytes 442372 | tf_op jit(solution)/shard_map/jit(dynamic_update_index_in_dim)/dynamic_update_slice | solution.py:222
  373.5 6.8 %dynamic_update_slice.54 = f32[4,96,576]{1,0,2:T(4,128)S(1)} dynamic-update-slice(f32[4,96,576]{1,0,2:T(4,128)S(1)} %dynamic_update_slice.53, f32[1,96,576]{1,0,2:T(1,128)S(1)} %copy.71, s32[]{:T(128)S(6)} %select_n.116, s32[]{:T(128)} %constant.137.clone.1, s32[]{:T(128)} %constant.137.clone.1) | dynamic-update-slice | bytes 442372 | tf_op jit(solution)/shard_map/jit(dynamic_update_index_in_dim)/dynamic_update_slice | solution.py:222
  (385 shorter events, 181.7 us)
Async XLA Ops:
  4.0 28.9 %collective-permute-start.2 = (bf16[512,768]{1,0:T(8,128)(2,1)S(1)}, bf16[512,768]{1,0:T(8,128)(2,1)S(1)}, u32[]{:S(2)}, u32[]{:S(2)}) collective-permute-start(bf16[512,768]{1,0:T(8,128)(2,1)S(1)} %fusion.21), channel_id=1, source_target_pairs={{0,2},{1,3},{2,0},{3,1},{4,6},{5,7},{6,4},{7,5},{8,10},{9,11},{10,... | collective-permute-start | bytes 2359304 | tf_op jit(solution)/shard_map/ppermute | solution.py:177
  7.1 31.4 %collective-permute-start.1 = (bf16[512,768]{1,0:T(8,128)(2,1)S(1)}, bf16[512,768]{1,0:T(8,128)(2,1)}, u32[]{:S(2)}, u32[]{:S(2)}) collective-permute-start(bf16[512,768]{1,0:T(8,128)(2,1)S(1)} %fusion.21), channel_id=1, source_target_pairs={{0,1},{1,0},{2,3},{3,2},{4,5},{5,4},{6,7},{7,6},{8,9},{9,8},{10,11... | collective-permute-start | bytes 2359304 | tf_op jit(solution)/shard_map/ppermute | solution.py:177
  7.1 24.0 %collective-permute-start = (bf16[384,576]{0,1:T(8,128)(2,1)}, bf16[384,576]{0,1:T(8,128)(2,1)}, u32[]{:S(2)}, u32[]{:S(2)}) collective-permute-start(bf16[384,576]{0,1:T(8,128)(2,1)} %bitcast.2), channel_id=1, source_target_pairs={{0,4},{4,0},{1,5},{5,1},{2,6},{6,2},{3,7},{7,3},{8,12},{12,8},{9,1... | collective-permute-start | bytes 1327112 | tf_op jit(solution)/shard_map/ppermute | solution.py:177
  31.1 27.9 %collective-permute-start.21 = (bf16[512,768]{1,0:T(8,128)(2,1)}, bf16[512,768]{1,0:T(8,128)(2,1)S(1)}, u32[]{:S(2)}, u32[]{:S(2)}) collective-permute-start(bf16[512,768]{1,0:T(8,128)(2,1)} %param.27), channel_id=1, source_target_pairs={{0,2},{1,3},{2,0},{3,1},{4,6},{5,7},{6,4},{7,5},{8,10},{9,11},{10,... | collective-permute-start | bytes 2359304 | tf_op jit(solution)/shard_map/ppermute | solution.py:177
  34.7 22.3 %collective-permute-start.12 = (bf16[384,768]{1,0:T(8,128)(2,1)S(1)}, bf16[384,768]{1,0:T(8,128)(2,1)S(1)}, u32[]{:S(2)}, u32[]{:S(2)}) collective-permute-start(bf16[384,768]{1,0:T(8,128)(2,1)S(1)} %copy-done.17), channel_id=1, source_target_pairs={{0,4},{4,0},{1,5},{5,1},{2,6},{6,2},{3,7},{7,3},{8,12},{12,8},{9,1... | collective-permute-start | bytes 1769480 | tf_op jit(solution)/shard_map/ppermute | solution.py:177
  36.3 22.0 %collective-permute-start.10 = (bf16[192,768]{1,0:T(8,128)(2,1)}, bf16[192,768]{1,0:T(8,128)(2,1)S(1)}, u32[]{:S(2)}, u32[]{:S(2)}) collective-permute-start(bf16[192,768]{1,0:T(8,128)(2,1)} %collective-permute-done.9), channel_id=1, source_target_pairs={{0,1},{1,0},{2,3},{3,2},{4,5},{5,4},{6,7},{7,6},{8,9},{9,8},{10,11... | collective-permute-start | bytes 884744 | tf_op jit(solution)/shard_map/ppermute | solution.py:177
  58.3 17.8 %collective-permute-start.19 = (bf16[512,768]{1,0:T(8,128)(2,1)}, bf16[512,768]{1,0:T(8,128)(2,1)S(1)}, u32[]{:S(2)}, u32[]{:S(2)}) collective-permute-start(bf16[512,768]{1,0:T(8,128)(2,1)} %param.27), channel_id=1, source_target_pairs={{0,1},{1,0},{2,3},{3,2},{4,5},{5,4},{6,7},{7,6},{8,9},{9,8},{10,11... | collective-permute-start | bytes 2359304 | tf_op jit(solution)/shard_map/ppermute | solution.py:177
  59.0 15.5 %collective-permute-start.13 = (bf16[768,384]{0,1:T(8,128)(2,1)}, bf16[768,384]{0,1:T(8,128)(2,1)S(1)}, u32[]{:S(2)}, u32[]{:S(2)}) collective-permute-start(bf16[768,384]{0,1:T(8,128)(2,1)} %copy.64), channel_id=1, source_target_pairs={{0,4},{4,0},{1,5},{5,1},{2,6},{6,2},{3,7},{7,3},{8,12},{12,8},{9,1... | collective-permute-start | bytes 1769480 | tf_op jit(solution)/shard_map/ppermute | solution.py:177
  59.6 18.1 %collective-permute-start.22 = (bf16[512,768]{1,0:T(8,128)(2,1)S(1)}, bf16[512,768]{1,0:T(8,128)(2,1)S(1)}, u32[]{:S(2)}, u32[]{:S(2)}) collective-permute-start(bf16[512,768]{1,0:T(8,128)(2,1)S(1)} %collective-permute-done.21), channel_id=1, source_target_pairs={{0,1},{1,0},{2,3},{3,2},{4,5},{5,4},{6,7},{7,6},{8,9},{9,8},{10,11... | collective-permute-start | bytes 2359304 | tf_op jit(solution)/shard_map/ppermute | solution.py:177
  69.0 20.4 %collective-permute-start.15 = (bf16[512,768]{1,0:T(8,128)(2,1)S(1)}, bf16[512,768]{1,0:T(8,128)(2,1)S(1)}, u32[]{:S(2)}, u32[]{:S(2)}) collective-permute-start(bf16[512,768]{1,0:T(8,128)(2,1)S(1)} %add_convert_fusion.6), channel_id=1, source_target_pairs={{0,2},{1,3},{2,0},{3,1},{4,6},{5,7},{6,4},{7,5},{8,10},{9,11},{10,... | collective-permute-start | bytes 2359304 | tf_op jit(solution)/shard_map/ppermute | solution.py:177
  69.6 19.8 %collective-permute-start.11 = (bf16[512,768]{1,0:T(8,128)(2,1)S(1)}, bf16[512,768]{1,0:T(8,128)(2,1)S(1)}, u32[]{:S(2)}, u32[]{:S(2)}) collective-permute-start(bf16[512,768]{1,0:T(8,128)(2,1)S(1)} %add_convert_fusion.6), channel_id=1, source_target_pairs={{0,1},{1,0},{2,3},{3,2},{4,5},{5,4},{6,7},{7,6},{8,9},{9,8},{10,11... | collective-permute-start | bytes 2359304 | tf_op jit(solution)/shard_map/ppermute | solution.py:177
  101.6 25.8 %collective-permute-start.74 = (bf16[384,768]{1,0:T(8,128)(2,1)S(1)}, bf16[384,768]{1,0:T(8,128)(2,1)S(1)}, u32[]{:S(2)}, u32[]{:S(2)}) collective-permute-start(bf16[384,768]{1,0:T(8,128)(2,1)S(1)} %fusion.34), channel_id=1, source_target_pairs={{0,4},{4,0},{1,5},{5,1},{2,6},{6,2},{3,7},{7,3},{8,12},{12,8},{9,1... | collective-permute-start | bytes 1769480 | tf_op jit(solution)/shard_map/ppermute | solution.py:177
  119.2 14.7 %collective-permute-start.64 = (bf16[384,768]{1,0:T(8,128)(2,1)S(1)}, bf16[384,768]{1,0:T(8,128)(2,1)S(1)}, u32[]{:S(2)}, u32[]{:S(2)}) collective-permute-start(bf16[384,768]{1,0:T(8,128)(2,1)S(1)} %fusion.33), channel_id=1, source_target_pairs={{0,4},{4,0},{1,5},{5,1},{2,6},{6,2},{3,7},{7,3},{8,12},{12,8},{9,1... | collective-permute-start | bytes 1769480 | tf_op jit(solution)/shard_map/ppermute | solution.py:177
  125.2 31.4 %collective-permute-start.17 = (bf16[512,768]{1,0:T(8,128)(2,1)S(1)}, bf16[512,768]{1,0:T(8,128)(2,1)S(1)}, u32[]{:S(2)}, u32[]{:S(2)}) collective-permute-start(bf16[512,768]{1,0:T(8,128)(2,1)S(1)} %slice.144), channel_id=1, source_target_pairs={{0,1},{1,0},{2,3},{3,2},{4,5},{5,4},{6,7},{7,6},{8,9},{9,8},{10,11... | collective-permute-start | bytes 2359304 | tf_op jit(solution)/shard_map/ppermute | solution.py:177
  126.3 34.0 %collective-permute-start.23 = (bf16[512,768]{1,0:T(8,128)(2,1)S(1)}, bf16[512,768]{1,0:T(8,128)(2,1)S(1)}, u32[]{:S(2)}, u32[]{:S(2)}) collective-permute-start(bf16[512,768]{1,0:T(8,128)(2,1)S(1)} %slice.148), channel_id=1, source_target_pairs={{0,1},{1,0},{2,3},{3,2},{4,5},{5,4},{6,7},{7,6},{8,9},{9,8},{10,11... | collective-permute-start | bytes 2359304 | tf_op jit(solution)/shard_map/ppermute | solution.py:177
  129.3 14.9 %collective-permute-start.76 = (bf16[96,768]{1,0:T(8,128)(2,1)S(1)}, bf16[96,768]{1,0:T(8,128)(2,1)S(1)}, u32[]{:S(2)}, u32[]{:S(2)}) collective-permute-start(bf16[96,768]{1,0:T(8,128)(2,1)S(1)} %get-tuple-element.88), channel_id=1, source_target_pairs={{0,16},{8,24},{16,0},{24,8},{1,17},{9,25},{17,1},{25,9},{2,18},{10... | collective-permute-start | bytes 442376 | tf_op jit(solution)/shard_map/ppermute | solution.py:177
  146.7 50.7 %collective-permute-start.31 = (bf16[768,576]{0,1:T(8,128)(2,1)S(1)}, bf16[768,576]{0,1:T(8,128)(2,1)}, u32[]{:S(2)}, u32[]{:S(2)}) collective-permute-start(bf16[768,576]{0,1:T(8,128)(2,1)S(1)} %bitcast.201), channel_id=1, source_target_pairs={{0,2},{1,3},{2,0},{3,1},{4,6},{5,7},{6,4},{7,5},{8,10},{9,11},{10,... | collective-permute-start | bytes 2654216 | tf_op jit(solution)/shard_map/ppermute | solution.py:177
  155.2 45.6 %collective-permute-start.14 = (bf16[512,768]{1,0:T(8,128)(2,1)}, bf16[512,768]{1,0:T(8,128)(2,1)}, u32[]{:S(2)}, u32[]{:S(2)}) collective-permute-start(bf16[512,768]{1,0:T(8,128)(2,1)} %slice.142), channel_id=1, source_target_pairs={{0,1},{1,0},{2,3},{3,2},{4,5},{5,4},{6,7},{7,6},{8,9},{9,8},{10,11... | collective-permute-start | bytes 2359304 | tf_op jit(solution)/shard_map/ppermute | solution.py:177
  155.2 42.3 %collective-permute-start.20 = (bf16[512,768]{1,0:T(8,128)(2,1)}, bf16[512,768]{1,0:T(8,128)(2,1)}, u32[]{:S(2)}, u32[]{:S(2)}) collective-permute-start(bf16[512,768]{1,0:T(8,128)(2,1)} %slice.146), channel_id=1, source_target_pairs={{0,1},{1,0},{2,3},{3,2},{4,5},{5,4},{6,7},{7,6},{8,9},{9,8},{10,11... | collective-permute-start | bytes 2359304 | tf_op jit(solution)/shard_map/ppermute | solution.py:177
  174.6 23.4 %collective-permute-start.24 = (bf16[512,768]{1,0:T(8,128)(2,1)}, bf16[512,768]{1,0:T(8,128)(2,1)}, u32[]{:S(2)}, u32[]{:S(2)}) collective-permute-start(bf16[512,768]{1,0:T(8,128)(2,1)} %add_convert_fusion.3), channel_id=1, source_target_pairs={{0,2},{1,3},{2,0},{3,1},{4,6},{5,7},{6,4},{7,5},{8,10},{9,11},{10,... | collective-permute-start | bytes 2359304 | tf_op jit(solution)/shard_map/ppermute | solution.py:177
  195.5 16.3 %collective-permute-start.18 = (bf16[512,768]{1,0:T(8,128)(2,1)}, bf16[512,768]{1,0:T(8,128)(2,1)S(1)}, u32[]{:S(2)}, u32[]{:S(2)}) collective-permute-start(bf16[512,768]{1,0:T(8,128)(2,1)} %add_convert_fusion.5), channel_id=1, source_target_pairs={{0,2},{1,3},{2,0},{3,1},{4,6},{5,7},{6,4},{7,5},{8,10},{9,11},{10,... | collective-permute-start | bytes 2359304 | tf_op jit(solution)/shard_map/ppermute | solution.py:177
  197.5 108.5 %collective-permute-start.29 = (bf16[768,576]{0,1:T(8,128)(2,1)S(1)}, bf16[768,576]{0,1:T(8,128)(2,1)}, u32[]{:S(2)}, u32[]{:S(2)}) collective-permute-start(bf16[768,576]{0,1:T(8,128)(2,1)S(1)} %bitcast.202), channel_id=1, source_target_pairs={{0,1},{1,0},{2,3},{3,2},{4,5},{5,4},{6,7},{7,6},{8,9},{9,8},{10,11... | collective-permute-start | bytes 2654216 | tf_op jit(solution)/shard_map/ppermute | solution.py:177
  197.6 110.7 %collective-permute-start.33 = (bf16[768,576]{0,1:T(8,128)(2,1)}, bf16[768,576]{0,1:T(8,128)(2,1)}, u32[]{:S(2)}, u32[]{:S(2)}) collective-permute-start(bf16[768,576]{0,1:T(8,128)(2,1)} %collective-permute-done.31), channel_id=1, source_target_pairs={{0,1},{1,0},{2,3},{3,2},{4,5},{5,4},{6,7},{7,6},{8,9},{9,8},{10,11... | collective-permute-start | bytes 2654216 | tf_op jit(solution)/shard_map/ppermute | solution.py:177
  223.7 44.4 %collective-permute-start.49 = (bf16[192,768]{1,0:T(8,128)(2,1)}, bf16[192,768]{1,0:T(8,128)(2,1)}, u32[]{:S(2)}, u32[]{:S(2)}) collective-permute-start(bf16[192,768]{1,0:T(8,128)(2,1)} %get-tuple-element.92), channel_id=1, source_target_pairs={{0,1},{1,0},{2,3},{3,2},{4,5},{5,4},{6,7},{7,6},{8,9},{9,8},{10,11... | collective-permute-start | bytes 884744 | tf_op jit(solution)/shard_map/ppermute | solution.py:177
  226.2 42.3 %collective-permute-start.50 = (bf16[192,768]{1,0:T(8,128)(2,1)}, bf16[192,768]{1,0:T(8,128)(2,1)}, u32[]{:S(2)}, u32[]{:S(2)}) collective-permute-start(bf16[192,768]{1,0:T(8,128)(2,1)} %get-tuple-element.94), channel_id=1, source_target_pairs={{0,2},{1,3},{2,0},{3,1},{4,6},{5,7},{6,4},{7,5},{8,10},{9,11},{10,... | collective-permute-start | bytes 884744 | tf_op jit(solution)/shard_map/ppermute | solution.py:177
  229.6 39.0 %collective-permute-start.51 = (bf16[192,768]{1,0:T(8,128)(2,1)}, bf16[192,768]{1,0:T(8,128)(2,1)}, u32[]{:S(2)}, u32[]{:S(2)}) collective-permute-start(bf16[192,768]{1,0:T(8,128)(2,1)} %get-tuple-element.93), channel_id=1, source_target_pairs={{0,3},{1,2},{2,1},{3,0},{4,7},{5,6},{6,5},{7,4},{8,11},{9,10},{10,... | collective-permute-start | bytes 884744 | tf_op jit(solution)/shard_map/ppermute | solution.py:177
  300.0 15.6 %collective-permute-start.32 = (bf16[576,512]{1,0:T(8,128)(2,1)}, bf16[576,512]{1,0:T(8,128)(2,1)S(1)}, u32[]{:S(2)}, u32[]{:S(2)}) collective-permute-start(bf16[576,512]{1,0:T(8,128)(2,1)} %get-tuple-element.82), channel_id=1, source_target_pairs={{0,3},{1,2},{2,1},{3,0},{4,7},{5,6},{6,5},{7,4},{8,11},{9,10},{10,... | collective-permute-start | bytes 1769480 | tf_op jit(solution)/shard_map/ppermute | solution.py:177
  303.1 31.5 %collective-permute-start.58 = (bf16[48,384]{1,0:T(8,128)(2,1)S(1)}, bf16[48,384]{1,0:T(8,128)(2,1)S(1)}, u32[]{:S(2)}, u32[]{:S(2)}) collective-permute-start(bf16[48,384]{1,0:T(8,128)(2,1)S(1)} %get-tuple-element.77), channel_id=1, source_target_pairs={{0,24},{8,16},{16,8},{24,0},{1,25},{9,17},{17,9},{25,1},{2,26},{10... | collective-permute-start | bytes 110600 | tf_op jit(solution)/shard_map/ppermute | solution.py:177
  337.9 16.0 %collective-permute-start.38 = (f32[2,768]{1,0:T(2,128)S(1)}, f32[2,768]{1,0:T(2,128)S(1)}, u32[]{:S(2)}, u32[]{:S(2)}) collective-permute-start(f32[2,768]{1,0:T(2,128)S(1)} %add.359), channel_id=1, source_target_pairs={{0,16},{8,24},{16,0},{24,8},{1,17},{9,25},{17,1},{25,9},{2,18},{10... | collective-permute-start | bytes 18440 | tf_op jit(solution)/shard_map/ppermute | solution.py:177
  341.9 17.3 %collective-permute-start.43 = (bf16[96,576]{1,0:T(8,128)(2,1)S(1)}, bf16[96,576]{1,0:T(8,128)(2,1)S(1)}, u32[]{:S(2)}, u32[]{:S(2)}) collective-permute-start(bf16[96,576]{1,0:T(8,128)(2,1)S(1)} %get-tuple-element.79), channel_id=1, source_target_pairs={{0,8},{8,0},{16,24},{24,16},{1,9},{9,1},{17,25},{25,17},{2,10},{10... | collective-permute-start | bytes 331784 | tf_op jit(solution)/shard_map/ppermute | solution.py:177
  344.1 15.2 %collective-permute-start.44 = (bf16[96,576]{1,0:T(8,128)(2,1)S(1)}, bf16[96,576]{1,0:T(8,128)(2,1)S(1)}, u32[]{:S(2)}, u32[]{:S(2)}) collective-permute-start(bf16[96,576]{1,0:T(8,128)(2,1)S(1)} %get-tuple-element.79), channel_id=1, source_target_pairs={{0,16},{8,24},{16,0},{24,8},{1,17},{9,25},{17,1},{25,9},{2,18},{10... | collective-permute-start | bytes 331784 | tf_op jit(solution)/shard_map/ppermute | solution.py:177
  344.1 15.5 %collective-permute-start.45 = (bf16[96,576]{1,0:T(8,128)(2,1)S(1)}, bf16[96,576]{1,0:T(8,128)(2,1)S(1)}, u32[]{:S(2)}, u32[]{:S(2)}) collective-permute-start(bf16[96,576]{1,0:T(8,128)(2,1)S(1)} %get-tuple-element.79), channel_id=1, source_target_pairs={{0,24},{8,16},{16,8},{24,0},{1,25},{9,17},{17,9},{25,1},{2,26},{10... | collective-permute-start | bytes 331784 | tf_op jit(solution)/shard_map/ppermute | solution.py:177
  (93 other events, 697.3 us)
